TPU v7x, 32 devices: a whole 2x2x4 slice. The times are simulated.
32 devices in a mesh: dp: 4 (over y, core), ep: 8 (over z, x).
Axes of the slice: x: 2, y: 2, z: 4, core: 2. Of those that a mesh axis runs over, the one named last changes fastest.
Arguments:
- tokens: bfloat16 [4096, 2048], P(('dp', 'ep')), may hold values from -6 to 6
- expert_ids: int32 [4096, 6], P(('dp', 'ep')), may hold values from 0 to 63, all different within a row; in each aligned block of 128 rows (0 to 127, 128 to 255, ...) at most 13 rows name the same one
- gate_scales: float32 [4096, 6], P(('dp', 'ep')), may hold values from 0.05 to 0.5
- expert_slot: int32 [64], replicated, may hold values from 0 to 63, each once
- gate_weight: bfloat16 [64, 2048, 1408], P('ep', 'dp'), may hold values from -0.125 to 0.125
- up_weight: bfloat16 [64, 2048, 1408], P('ep', 'dp'), may hold values from -0.125 to 0.125
- down_weight: bfloat16 [64, 1408, 2048], P('ep', None, 'dp'), may hold values from -0.15625 to 0.15625
Outputs:
- mixed: bfloat16 [4096, 2048], P(('dp', 'ep'))
Inputs may be any that keep to these rules, and one draw needn't show every extreme that they name: `expert_ids`: among the 128 tokens of one device no expert is chosen by more than 13; the 6 experts of a token differ. `expert_slot`: each expert has exactly one slot.
All inputs are finite; a program needn't handle non-finite values.
Results may differ from a plain program's by a relative error of at most 0.0057.
Values may be sent and summed in bfloat16 or wider, within the bound.
A program may use at most 256 MiB of HBM per device.

v0:
```python
import jax
import jax.numpy as jnp
from jax import lax
from jax.sharding import PartitionSpec as P

C = 13


def local(tokens, expert_ids, gate_scales, expert_slot, gate_weight, up_weight, down_weight):
    tok_rows = tokens.shape[0]
    width = tokens.shape[1]
    top = expert_ids.shape[1]
    experts = expert_slot.shape[0]
    exp_dev = gate_weight.shape[0]
    n_ep = lax.axis_size("ep")
    capacity = C
    ids = expert_ids.reshape(-1)
    onehot = (ids[:, None] == jnp.arange(experts, dtype=jnp.int32)[None, :]).astype(jnp.int32)
    earlier = jnp.cumsum(onehot, 0) - onehot
    rank = jnp.sum(earlier * onehot, 1)
    target = jnp.sum(onehot * expert_slot[None, :], 1)
    flat_slot = target * capacity + rank
    sources = jnp.repeat(tokens, top, axis=0)
    send = jnp.zeros((experts * capacity, width), jnp.bfloat16).at[flat_slot].set(sources)
    send = send.reshape(n_ep, exp_dev, capacity, width)
    received = lax.all_to_all(send, "ep", split_axis=0, concat_axis=0, tiled=True)
    gate = jnp.einsum(
        "secd,edf->secf",
        received,
        lax.all_gather(gate_weight, "dp", axis=1, tiled=True),
        preferred_element_type=jnp.float32,
    )
    up = jnp.einsum(
        "secd,edf->secf",
        received,
        lax.all_gather(up_weight, "dp", axis=1, tiled=True),
        preferred_element_type=jnp.float32,
    )
    gate, up = (gate, up)
    hidden = (jax.nn.silu(gate) * up).astype(jnp.bfloat16)
    expert_out = jnp.einsum(
        "secf,efd->secd",
        hidden,
        lax.all_gather(down_weight, "dp", axis=2, tiled=True),
        preferred_element_type=jnp.float32,
    ).astype(jnp.bfloat16)
    returned = lax.all_to_all(expert_out, "ep", split_axis=0, concat_axis=0, tiled=True)
    returned = returned.reshape(experts * capacity, width)
    picked = returned[flat_slot].reshape(tok_rows, top, width)
    mixed = jnp.sum(gate_scales[:, :, None] * picked.astype(jnp.float32), 1)
    return mixed.astype(jnp.bfloat16)


def solution(mesh):
    in_specs = (
        P(("dp", "ep"), None),
        P(("dp", "ep"), None),
        P(("dp", "ep"), None),
        P(),
        P("ep", "dp", None),
        P("ep", "dp", None),
        P("ep", None, "dp"),
    )
    out_specs = P(("dp", "ep"), None)
    return jax.shard_map(local, mesh=mesh, in_specs=in_specs, out_specs=out_specs, check_vma=False)
```

profile of v0, /device:TPU:0, one launch (start us, length us, event | category | flops | bytes accessed | tf_op | source)
XLA Modules:
  0.0 970.3 jit_solution(5649581719288517447)
XLA Ops:
  6.5 0.7 all-gather.6.cloned.1.call-update
  7.3 0.0 all-gather.4.cloned.1.call-start
  7.3 0.7 all-gather.4.cloned.1.call-update
  8.0 0.0 all-gather.8.cloned.1.call-start
  8.1 0.7 all-gather.8.cloned.1.call-update
  8.8 0.1 copy.16
  8.9 0.1 eq.29
  9.0 0.1 eq.25
  9.2 1.8 reduce-window.6
  11.0 0.3 slice_reduce_fusion
  11.3 2.6 broadcast_in_dim.5
  13.9 6.4 reshape.74
  20.4 0.1 select_reduce_fusion
  20.6 9.6 scatter_custom_fusion
  30.2 2.9 reshape.59
  33.1 5.5 copy.19
  38.6 83.7 %all_to_all.10 = bf16[8,8,13,2048]{3,1,2,0:T(8,128)(2,1)S(1)} all-to-all(bf16[8,8,13,2048]{3,1,2,0:T(8,128)(2,1)S(1)} %copy.19), channel_id=1, replica_groups=mesh['dp'=4,'ep'=8] {'ep'}, dimensions={0} | all-to-all | bytes 6815744 | tf_op jit(solution)/shard_map/all_to_all | solution.py:26
  122.3 162.7 %all-gather.6.cloned.1.call-done = bf16[8,2048,1408]{2,1,0:T(8,128)(2,1)} async-done(((bf16[8,512,1408]{2,1,0:T(8,128)(2,1)}), bf16[8,2048,1408]{2,1,0:T(8,128)(2,1)}) %all-gather.6.cloned.1.call-update) | async-done | bytes 46137360 | tf_op jit(solution)/shard_map/all_gather | solution.py:36
  285.0 28.6 %fusion.2 = f32[8,8,13,1408]{3,2,1,0:T(8,128)} fusion(bf16[8,2048,1408]{2,1,0:T(8,128)(2,1)} %all-gather.6.cloned.1.call-done, bf16[8,8,13,2048]{3,1,2,0:T(8,128)(2,1)S(1)} %all_to_all.10), kind=kOutput, calls=%fused_computation.4 | convolution fusion | flops 4798283776 | bytes 54231040 | tf_op jit(solution)/shard_map/secd,edf->secf/dot_general | solution.py:33
  313.6 246.3 %all-gather.4.cloned.1.call-done = bf16[8,2048,1408]{2,1,0:T(8,128)(2,1)} async-done(((bf16[8,512,1408]{2,1,0:T(8,128)(2,1)}), bf16[8,2048,1408]{2,1,0:T(8,128)(2,1)}) %all-gather.4.cloned.1.call-update) | async-done | bytes 46137360 | tf_op jit(solution)/shard_map/all_gather | solution.py:30
  559.9 32.0 %fusion.6 = bf16[8,8,13,1408]{3,2,0,1:T(8,128)(2,1)S(1)} fusion(f32[8,8,13,1408]{3,2,1,0:T(8,128)} %fusion.2, bf16[8,2048,1408]{2,1,0:T(8,128)(2,1)} %all-gather.4.cloned.1.call-done, bf16[8,8,13,2048]{3,1,2,0:T(8,128)(2,1)} %copy-done), kind=kOutput, calls=%fused_computation.10 | convolution fusion | flops 4805312512 | bytes 56573952 | tf_op jit(solution)/shard_map/secd,edf->secf/dot_general | solution.py:27
  591.9 243.2 %all-gather.8.cloned.1.call-done = bf16[8,1408,2048]{2,1,0:T(8,128)(2,1)} async-done(((bf16[8,1408,512]{2,1,0:T(8,128)(2,1)}), bf16[8,1408,2048]{2,1,0:T(8,128)(2,1)}) %all-gather.8.cloned.1.call-update) | async-done | bytes 46137360 | tf_op jit(solution)/shard_map/all_gather | solution.py:44
  835.2 16.6 %convert_bitcast_fusion = bf16[8,8,13,2048]{3,2,0,1:T(8,128)(2,1)S(1)} fusion(bf16[8,8,13,1408]{3,2,0,1:T(8,128)(2,1)S(1)} %fusion.6, bf16[8,1408,2048]{2,1,0:T(8,128)(2,1)} %all-gather.8.cloned.1.call-done), kind=kOutput, calls=%fused_computation.16 | convolution fusion | flops 4799987712 | bytes 51888128 | tf_op jit(solution)/shard_map/secf,efd->secd/dot_general | solution.py:41
  851.8 3.8 copy.22
  855.6 5.6 all-to-all-start.1
  861.3 0.1 copy.15
  861.4 76.6 %all-to-all-done.1 = bf16[8,8,13,2048]{3,1,2,0:T(8,128)(2,1)S(1)} async-done(((bf16[8,8,13,2048]{3,1,2,0:T(8,128)(2,1)}), bf16[8,8,13,2048]{3,1,2,0:T(8,128)(2,1)S(1)}, u32[]{:S(2)}, u32[]{:S(2)}) %all-to-all-start.1) | async-done | bytes 3407904 | tf_op jit(solution)/shard_map/all_to_all | solution.py:47
  938.0 4.0 copy.23
  942.0 3.4 reshape.60
  945.5 4.3 gather_fusion
  949.8 6.6 reshape.61
  956.3 7.4 multiply_reduce_fusion
  (16 shorter events, 0.1 us)
Async XLA Ops:
  6.5 278.5 %all-gather.6.cloned.1.call-start = ((), (), s32[]{:S(2)}) async-start(), calls=%async_computation.3 | async-start | bytes 57671680 | tf_op jit(solution)/shard_map/all_gather | solution.py:36
  7.3 552.7 %all-gather.4.cloned.1.call-start = ((), (), s32[]{:S(2)}) async-start(), calls=%async_computation.2 | async-start | bytes 57671680 | tf_op jit(solution)/shard_map/all_gather | solution.py:30
  8.0 0.8 copy-start.2
  8.0 3.3 copy-start.1
  8.0 827.1 %all-gather.8.cloned.1.call-start = ((), (), s32[]{:S(2)}) async-start(), calls=%async_computation.4 | async-start | bytes 57671680 | tf_op jit(solution)/shard_map/all_gather | solution.py:44
  13.9 6.4 copy-start.4
  122.3 191.3 %copy-start = (bf16[8,8,13,2048]{3,1,2,0:T(8,128)(2,1)}, bf16[8,8,13,2048]{3,1,2,0:T(8,128)(2,1)S(1)}, u32[]{:S(2)}) copy-start(bf16[8,8,13,2048]{3,1,2,0:T(8,128)(2,1)S(1)} %all_to_all.10) | copy-start | bytes 10223620
  855.6 5.7 copy-start.3
  855.6 82.4 %all-to-all-start.1 = ((bf16[8,8,13,2048]{3,1,2,0:T(8,128)(2,1)}), bf16[8,8,13,2048]{3,1,2,0:T(8,128)(2,1)S(1)}, u32[]{:S(2)}, u32[]{:S(2)}) async-start(bf16[8,8,13,2048]{3,1,2,0:T(8,128)(2,1)} %copy.22), calls=%async_computation.1 | async-start | bytes 6815744 | tf_op jit(solution)/shard_map/all_to_all | solution.py:47
Sparse Core Ops, SparseCore 0:
  8.9 276.0 all-gather.5
  286.6 273.3 all-gather.3
  561.5 273.5 all-gather.7
where the time goes:
time: 971 us; the launch traced here: 970 us
  waiting for transfers between devices  731 us (75%)
  blocking collectives  83.7 us (9%)
  matrix products  77.3 us (8%)
  local copies, waits for them, and re-layouts  50 us (5%)
  between operations  13.2 us (1%)
    all_gather x1, waiting for transfers between devices, local(): lax.all_gather(gate_weight, 'dp', axis=1, tiled=True)  246 us
    all_gather x1, waiting for transfers between devices, local(): lax.all_gather(down_weight, 'dp', axis=2, tiled=True)  243 us
    all_gather x1, waiting for transfers between devices, local(): lax.all_gather(up_weight, 'dp', axis=1, tiled=True)  163 us
    all_to_all x1, blocking collectives, local(): lax.all_to_all(send, 'ep', split_axis=0, concat_axis=0, tiled=True)  83.7 us
    all_to_all x1, waiting for transfers between devices, local(): lax.all_to_all(expert_out, 'ep', split_axis=0, concat_axis=0, tiled=True)  76.6 us
    dot_general x1, matrix products, local(): jnp.einsum('secd,edf->secf', received, lax.all_gather(gate_weight, 'dp',...  32 us
    dot_general x1, matrix products, local(): jnp.einsum('secd,edf->secf', received, lax.all_gather(up_weight, 'dp', ax...  28.6 us
  transfers between devices with their start and end apart: 4, of which 4 were waited for; matrix products, arithmetic and copies ran while one was open for 9% of the time, Pallas kernels for 0%

commit v1 on v0

v1 whole, which is shorter than its diff:
```python
import jax
import jax.numpy as jnp
from jax import lax
from jax.sharding import PartitionSpec as P

C = 13
GROUP = 8
CHUNKS = 4
F32 = jnp.float32
BF16 = jnp.bfloat16


def local(tokens, expert_ids, gate_scales, expert_slot, gate_weight, up_weight, down_weight):
    tok = tokens.shape[0]
    top = expert_ids.shape[1]
    experts = expert_slot.shape[0]
    exp_dev, part_d, ff = gate_weight.shape
    n_dp = lax.axis_size("dp")
    n_ep = lax.axis_size("ep")
    sources = n_dp * n_ep
    groups = sources // GROUP
    inner = groups // 4
    span = GROUP * tok
    rows = GROUP * C
    me_dp = lax.axis_index("dp")
    me_ep = lax.axis_index("ep")
    core, far = me_dp % 2, me_dp // 2
    over_core = [(i, i ^ 1) for i in range(4)]
    over_far = [(i, i ^ 2) for i in range(4)]

    def relative(a):
        a = a.reshape((2, 2) + a.shape[1:])
        a = jnp.where(core == 0, a, jnp.concatenate([a[:, 1:], a[:, :1]], 1))
        return jnp.where(far == 0, a, jnp.concatenate([a[1:], a[:1]], 0))

    mine = lax.all_to_all(tokens, "dp", split_axis=1, concat_axis=0, tiled=True)
    every = lax.all_gather(mine, "ep", axis=0, tiled=True)
    every = every.reshape(4, inner, span, part_d)

    same = expert_ids[:, :, None] == jnp.arange(experts, dtype=jnp.int32)
    slot = jnp.sum(jnp.where(same, expert_slot, 0), 2)
    meta = jnp.concatenate([gate_scales, slot.astype(F32)], 1).T
    meta = lax.all_gather(meta, ("ep", "dp"), axis=0)
    here = meta[:, top:].astype(jnp.int32) - me_ep * exp_dev
    hit = here[:, None] == jnp.arange(exp_dev, dtype=jnp.int32)[None, :, None, None]
    scale = jnp.sum(jnp.where(hit, meta[:, None, :top], 0.0), 2)
    chosen = jnp.any(hit, 2)
    before = jnp.triu(jnp.ones((tok, tok), BF16), 1)
    rank = jnp.einsum("set,tu->seu", chosen.astype(BF16), before, preferred_element_type=F32)
    base = (jnp.arange(sources, dtype=jnp.int32) % GROUP * C)[:, None, None]
    place = jnp.where(chosen, base + rank.astype(jnp.int32), -1)

    def by_group(a):
        a = a.reshape(4, inner, GROUP, exp_dev, tok)
        return jnp.swapaxes(a, 2, 3).reshape(4, inner, exp_dev, span)

    place, scale = by_group(place), by_group(scale)
    at = place[:, :, :, None, :] == jnp.arange(rows, dtype=jnp.int32)[:, None]

    sent = jnp.einsum("bgert,bgtd->bgerd", at.astype(BF16), every, preferred_element_type=F32).astype(BF16)
    sent = relative(sent)

    chunks = min(CHUNKS, exp_dev)
    per = exp_dev // chunks
    outs = []
    for i in range(chunks):
        own = slice(i * per, (i + 1) * per)
        picked = sent[:, :, :, own]

        def project(weight):
            def piece(x):
                return jnp.einsum("ygerd,edf->ygerf", x, weight[own], preferred_element_type=F32)

            got = lax.ppermute(piece(picked[:, 1]).astype(BF16), "dp", over_core)
            total = piece(picked[:, 0]) + got.astype(F32)
            got = lax.ppermute(total[1].astype(BF16), "dp", over_far)
            return total[0] + got.astype(F32)

        hidden = (jax.nn.silu(project(gate_weight)) * project(up_weight)).astype(BF16)
        other = lax.ppermute(hidden, "dp", over_far)
        pair = jnp.stack([hidden, other])
        hidden = jnp.stack([pair, jnp.stack([lax.ppermute(hidden, "dp", over_core), lax.ppermute(other, "dp", over_core)])], 1)
        outs.append(jnp.einsum("yxgerf,efd->yxgerd", hidden, down_weight[own], preferred_element_type=F32).astype(BF16))
    out = jnp.concatenate(outs, 3)
    out = relative(out.reshape((4,) + out.shape[2:])).reshape((4,) + out.shape[2:])

    weight = jnp.where(at, scale[:, :, :, None, :], 0.0)
    high = weight.astype(BF16)
    low = (weight - high.astype(F32)).astype(BF16)
    both = jnp.concatenate([high, low], 3)
    out = jnp.concatenate([out, out], 3)
    mixed = jnp.einsum("bgert,bgerd->bgtd", both, out, preferred_element_type=F32).astype(BF16)
    mixed = mixed.reshape(n_ep * n_dp * tok, part_d)
    mixed = lax.psum_scatter(mixed, "ep", scatter_dimension=0, tiled=True)
    mixed = lax.all_to_all(mixed, "dp", split_axis=0, concat_axis=1, tiled=True)
    return mixed.astype(BF16)


def solution(mesh):
    in_specs = (
        P(("dp", "ep"), None),
        P(("dp", "ep"), None),
        P(("dp", "ep"), None),
        P(),
        P("ep", "dp", None),
        P("ep", "dp", None),
        P("ep", None, "dp"),
    )
    out_specs = P(("dp", "ep"), None)
    return jax.shard_map(local, mesh=mesh, in_specs=in_specs, out_specs=out_specs, check_vma=False)
```

time: 971 us -> 418 us (0.43)
  waiting for transfers between devices: 731 us -> 236 us
  local copies, waits for them, and re-layouts: 50 us -> 7.93 us
  matrix products: 77.3 us -> 42.7 us
  blocking collectives: 83.7 us -> 68 us
  starting transfers between devices: 5.73 us -> 19.6 us
  other arithmetic: 9.4 us -> 20.1 us
    all_gather x3 -> x1, waiting for transfers between devices: 652 us -> 19.8 us  [local(): every = lax.all_gather(mine, 'ep', axis=0, tiled=True)]
    ppermute x0 -> x28, waiting for transfers between devices: none -> 130 us  [the longest x8 84.4 us: project(): got = lax.ppermute(total[1].astype(BF16), 'dp', over_far)]
    reduce_scatter x0 -> x1, waiting for transfers between devices: none -> 86.5 us  [local(): mixed = lax.psum_scatter(mixed, 'ep', scatter_dimension=0, tiled=True)]
    all_to_all x1 -> x0, waiting for transfers between devices: 76.6 us -> none  [local(): lax.all_to_all(expert_out, 'ep', split_axis=0, concat_axis=0, tiled=True)]
    all_to_all x1 -> x2, blocking collectives: 83.7 us -> 25.3 us  [the longest x1 13 us: local(): mine = lax.all_to_all(tokens, 'dp', split_axis=1, concat_axis=0, tiled=True)]
    all_gather x0 -> x1, blocking collectives: none -> 42.7 us  [local(): meta = lax.all_gather(meta, ('ep', 'dp'), axis=0)]
    dot_general x3 -> x23, matrix products: 77.3 us -> 42.7 us  [the longest x16 17.8 us: piece(): jnp.einsum('ygerd,edf->ygerf', x, weight[own], preferred_element_type=F32)]
    ppermute x0 -> x28, starting transfers between devices: none -> 19.6 us  [the longest x8 10.3 us: project(): got = lax.ppermute(total[1].astype(BF16), 'dp', over_far)]
  transfers between devices with their start and end apart: 4 -> 30, of which waited for: 4 -> 13; matrix products, arithmetic and copies ran while one was open for 9% -> 9% of each run, Pallas kernels for 0% -> 0%
where the time goes in v1:
time: 418 us; the launch traced here: 409 us
  waiting for transfers between devices  236 us (56%)
  blocking collectives  68 us (16%)
  matrix products  42.7 us (10%)
  other arithmetic  20.1 us (5%)
  starting transfers between devices  19.6 us (5%)
  between operations  14.6 us (3%)
  local copies, waits for them, and re-layouts  7.93 us (2%)
    reduce_scatter x1, waiting for transfers between devices, local(): mixed = lax.psum_scatter(mixed, 'ep', scatter_dimension=0, tiled=True)  86.5 us
    ppermute x8, waiting for transfers between devices, project(): got = lax.ppermute(total[1].astype(BF16), 'dp', over_far)  84.4 us
    ppermute x4, waiting for transfers between devices, local(): other = lax.ppermute(hidden, 'dp', over_far)  45.7 us
    all_gather x1, blocking collectives, local(): meta = lax.all_gather(meta, ('ep', 'dp'), axis=0)  42.7 us
    all_gather x1, waiting for transfers between devices, local(): every = lax.all_gather(mine, 'ep', axis=0, tiled=True)  19.8 us
    dot_general x16, matrix products, piece(): jnp.einsum('ygerd,edf->ygerf', x, weight[own], preferred_element_type=F32)  17.8 us
    all_to_all x1, blocking collectives, local(): mine = lax.all_to_all(tokens, 'dp', split_axis=1, concat_axis=0, tiled=True)  13 us
    dot_general x1, matrix products, local(): jnp.einsum('bgert,bgerd->bgtd', both, out, preferred_element_type=F32)  12.6 us
  transfers between devices with their start and end apart: 30, of which 13 were waited for; matrix products, arithmetic and copies ran while one was open for 9% of the time, Pallas kernels for 0%

profile of v1, /device:TPU:0, one launch (start us, length us, event | category | flops | bytes accessed | tf_op | source)
XLA Modules:
  0.0 409.4 jit_solution(3263479691235633417)
XLA Ops:
  8.1 13.0 %all_to_all.38 = bf16[128,4,512]{2,0,1:T(8,128)(2,1)} all-to-all(bf16[128,4,512]{2,0,1:T(8,128)(2,1)S(1)} %copy.143), channel_id=1, replica_groups=mesh['dp'=4,'ep'=8] {'dp'}, dimensions={1} | all-to-all | bytes 1048576 | tf_op jit(solution)/shard_map/all_to_all | solution.py:36
  21.4 42.7 %all-gather.1 = f32[32,12,128]{2,1,0:T(8,128)S(1)} all-gather(f32[1,12,128]{2,1,0:T(8,128)S(1)} %maximum_bitcast_fusion.20), channel_id=2, replica_groups=mesh['dp'=4,'ep'=8] {'ep','dp'}, dimensions={0}, use_global_device_ids=true | all-gather | bytes 202752 | tf_op jit(solution)/shard_map/all_gather | solution.py:43
  64.6 6.3 %select_convert_fusion = bf16[4,1,8,104,1024]{4,3,2,0,1:T(8,128)(2,1)} fusion(f32[4,8,1024]{2,1,0:T(8,128)S(1)} %bitcast.478, s32[4,8,1024]{2,1,0:T(8,128)S(1)} %bitcast.492), kind=kLoop, calls=%fused_computation.1 | loop fusion | flops 6815744 | bytes 7077888 | tf_op jit(solution)/shard_map/convert_element_type | solution.py:88
  70.9 5.6 %fusion = bf16[4,1,8,104,1024]{4,3,2,0,1:T(8,128)(2,1)} fusion(f32[4,8,1024]{2,1,0:T(8,128)S(1)} %bitcast.479, s32[4,8,1024]{2,1,0:T(8,128)S(1)} %bitcast.493), kind=kLoop, calls=%fused_computation.2 | loop fusion | flops 20447232 | bytes 7077888 | tf_op jit(solution)/shard_map/convert_element_type | solution.py:89
  76.4 19.8 %all-gather.4.cloned.1.call-done = bf16[4096,512]{1,0:T(8,128)(2,1)} async-done(((bf16[512,512]{1,0:T(8,128)(2,1)}), bf16[4096,512]{1,0:T(8,128)(2,1)}) %all-gather.4.cloned.1.call-update) | async-done | bytes 4194320 | tf_op jit(solution)/shard_map/all_gather | solution.py:37
  96.3 6.1 %fusion.109 = bf16[4,8,104,512]{3,2,1,0:T(8,128)(2,1)S(1)} fusion(bf16[4,1024,512,1]{2,1,3,0:T(8,128)(2,1)} %bitcast.498, s32[4,8,1024]{2,1,0:T(8,128)S(1)} %bitcast.494), kind=kOutput, calls=%fused_computation.99 | convolution fusion | flops 3494772736 | bytes 7733248 | tf_op jit(solution)/shard_map/bgert,bgtd->bgerd/dot_general | solution.py:60
  104.0 1.7 maximum_select_fusion.1
  109.0 1.9 fusion.78
  113.7 1.9 fusion.75
  115.8 1.8 fusion.69
  117.6 1.9 fusion.72
  124.0 1.5 collective-permute-start.1
  128.0 1.5 collective-permute-start.10
  132.2 1.5 collective-permute-start.17
  134.9 17.9 %collective-permute-done.8 = bf16[1,2,104,1408]{3,2,1,0:T(8,128)(2,1)S(1)} collective-permute-done((bf16[1,2,104,1408]{3,2,1,0:T(8,128)(2,1)S(1)}, bf16[1,2,104,1408]{3,2,1,0:T(8,128)(2,1)S(1)}, u32[]{:S(2)}, u32[]{:S(2)}) %collective-permute-start.8) | collective-permute-done | bytes 585760 | tf_op jit(solution)/shard_map/ppermute | solution.py:76
  154.2 11.1 %collective-permute-done.10 = bf16[1,2,104,1408]{3,2,1,0:T(8,128)(2,1)S(1)} collective-permute-done((bf16[1,2,104,1408]{3,2,1,0:T(8,128)(2,1)S(1)}, bf16[1,2,104,1408]{3,2,1,0:T(8,128)(2,1)S(1)}, u32[]{:S(2)}, u32[]{:S(2)}) %collective-permute-start.10) | collective-permute-done | bytes 585760 | tf_op jit(solution)/shard_map/ppermute | solution.py:76
  167.2 10.6 %collective-permute-done.15 = bf16[1,2,104,1408]{3,2,1,0:T(8,128)(2,1)S(1)} collective-permute-done((bf16[1,2,104,1408]{3,2,1,0:T(8,128)(2,1)S(1)}, bf16[1,2,104,1408]{3,2,1,0:T(8,128)(2,1)S(1)}, u32[]{:S(2)}, u32[]{:S(2)}) %collective-permute-start.15) | collective-permute-done | bytes 585760 | tf_op jit(solution)/shard_map/ppermute | solution.py:76
  179.3 11.1 %collective-permute-done.17 = bf16[1,2,104,1408]{3,2,1,0:T(8,128)(2,1)S(1)} collective-permute-done((bf16[1,2,104,1408]{3,2,1,0:T(8,128)(2,1)S(1)}, bf16[1,2,104,1408]{3,2,1,0:T(8,128)(2,1)S(1)}, u32[]{:S(2)}, u32[]{:S(2)}) %collective-permute-start.17) | collective-permute-done | bytes 585760 | tf_op jit(solution)/shard_map/ppermute | solution.py:76
  190.8 12.1 %collective-permute-done.22 = bf16[1,2,104,1408]{3,2,1,0:T(8,128)(2,1)S(1)} collective-permute-done((bf16[1,2,104,1408]{3,2,1,0:T(8,128)(2,1)S(1)}, bf16[1,2,104,1408]{3,2,1,0:T(8,128)(2,1)S(1)}, u32[]{:S(2)}, u32[]{:S(2)}) %collective-permute-start.22) | collective-permute-done | bytes 585760 | tf_op jit(solution)/shard_map/ppermute | solution.py:76
  204.4 11.1 %collective-permute-done.24 = bf16[1,2,104,1408]{3,2,1,0:T(8,128)(2,1)S(1)} collective-permute-done((bf16[1,2,104,1408]{3,2,1,0:T(8,128)(2,1)S(1)}, bf16[1,2,104,1408]{3,2,1,0:T(8,128)(2,1)S(1)}, u32[]{:S(2)}, u32[]{:S(2)}) %collective-permute-start.24) | collective-permute-done | bytes 585760 | tf_op jit(solution)/shard_map/ppermute | solution.py:76
  215.9 1.5 collective-permute-start.18
  217.5 10.6 %collective-permute-done.3 = bf16[1,2,104,1408]{3,2,1,0:T(8,128)(2,1)S(1)} collective-permute-done((bf16[1,2,104,1408]{3,2,1,0:T(8,128)(2,1)S(1)}, bf16[1,2,104,1408]{3,2,1,0:T(8,128)(2,1)S(1)}, u32[]{:S(2)}, u32[]{:S(2)}) %collective-permute-start.3) | collective-permute-done | bytes 585760 | tf_op jit(solution)/shard_map/ppermute | solution.py:76
  230.0 10.6 %collective-permute-done.11 = bf16[1,2,104,1408]{3,2,1,0:T(8,128)(2,1)S(1)} collective-permute-done((bf16[1,2,104,1408]{3,2,1,0:T(8,128)(2,1)S(1)}, bf16[1,2,104,1408]{3,2,1,0:T(8,128)(2,1)S(1)}, u32[]{:S(2)}, u32[]{:S(2)}) %collective-permute-start.11) | collective-permute-done | bytes 585760 | tf_op jit(solution)/shard_map/ppermute | solution.py:80
  242.2 10.9 %collective-permute-done.18 = bf16[1,2,104,1408]{3,2,1,0:T(8,128)(2,1)S(1)} collective-permute-done((bf16[1,2,104,1408]{3,2,1,0:T(8,128)(2,1)S(1)}, bf16[1,2,104,1408]{3,2,1,0:T(8,128)(2,1)S(1)}, u32[]{:S(2)}, u32[]{:S(2)}) %collective-permute-start.18) | collective-permute-done | bytes 585760 | tf_op jit(solution)/shard_map/ppermute | solution.py:80
  253.3 12.4 %collective-permute-done.25 = bf16[1,2,104,1408]{3,2,1,0:T(8,128)(2,1)S(1)} collective-permute-done((bf16[1,2,104,1408]{3,2,1,0:T(8,128)(2,1)S(1)}, bf16[1,2,104,1408]{3,2,1,0:T(8,128)(2,1)S(1)}, u32[]{:S(2)}, u32[]{:S(2)}) %collective-permute-start.25) | collective-permute-done | bytes 585760 | tf_op jit(solution)/shard_map/ppermute | solution.py:80
  265.8 11.7 %collective-permute-done.4 = bf16[1,2,104,1408]{3,2,1,0:T(8,128)(2,1)S(1)} collective-permute-done((bf16[1,2,104,1408]{3,2,1,0:T(8,128)(2,1)S(1)}, bf16[1,2,104,1408]{3,2,1,0:T(8,128)(2,1)S(1)}, u32[]{:S(2)}, u32[]{:S(2)}) %collective-permute-start.4) | collective-permute-done | bytes 585760 | tf_op jit(solution)/shard_map/ppermute | solution.py:80
  278.5 1.5 fusion.144
  280.7 1.5 fusion.139
  284.2 1.5 fusion.149
  289.4 12.6 %bitcast_convert_fusion = bf16[4,1024,512]{2,1,0:T(8,128)(2,1)} fusion(bf16[4,1,8,104,512]{4,3,2,0,1:T(8,128)(2,1)S(1)} %fusion.8, bf16[4,1,8,104,1024]{4,3,2,0,1:T(8,128)(2,1)} %fusion, bf16[4,1,8,104,1024]{4,3,2,0,1:T(8,128)(2,1)} %select_convert_fusion), kind=kOutput, calls=%fused_computation.10 | convolution fusion | flops 7022313472 | bytes 21233664 | tf_op jit(solution)/shard_map/bgert,bgerd->bgtd/dot_general | solution.py:92
  302.0 86.5 %reduce-scatter.2.cloned.1.call-done = bf16[512,512]{1,0:T(8,128)(2,1)} async-done(((bf16[4096,512]{1,0:T(8,128)(2,1)}), bf16[512,512]{1,0:T(8,128)(2,1)}) %reduce-scatter.2.cloned.1.call-update) | async-done | bytes 524304 | tf_op jit(solution)/shard_map/reduce_scatter | solution.py:94
  388.5 12.3 %all_to_all.39 = bf16[4,128,512]{2,1,0:T(8,128)(2,1)S(1)} all-to-all(bf16[4,128,512]{2,1,0:T(8,128)(2,1)} %bitcast.495), channel_id=1, replica_groups=mesh['dp'=4,'ep'=8] {'dp'}, dimensions={0} | all-to-all | bytes 1048576 | tf_op jit(solution)/shard_map/all_to_all | solution.py:95
  (134 shorter events, 39.9 us)
Async XLA Ops:
  6.5 89.7 %all-gather.4.cloned.1.call-start = ((), (), s32[]{:S(2)}) async-start(), calls=%async_computation.3 | async-start | bytes 4718592 | tf_op jit(solution)/shard_map/all_gather | solution.py:37
  21.1 367.4 %reduce-scatter.2.cloned.1.call-start = ((), (), s32[]{:S(2)}) async-start(), calls=%async_computation.4 | async-start | bytes 4718592 | tf_op jit(solution)/shard_map/reduce_scatter | solution.py:94
  108.9 11.4 %collective-permute-start = (bf16[2,1,2,104,1408]{4,3,0,2,1:T(8,128)(2,1)S(1)}, bf16[2,1,2,104,1408]{4,3,0,2,1:T(8,128)(2,1)S(1)}, u32[]{:S(2)}, u32[]{:S(2)}) collective-permute-start(bf16[2,1,2,104,1408]{4,3,0,2,1:T(8,128)(2,1)S(1)} %fusion.90), channel_id=1, source_target_pairs={{0,8},{8,0},{16,24},{24,16},{1,9},{9,1},{17,25},{25,17},{2,10},{10... | collective-permute-start | bytes 3514376 | tf_op jit(solution)/shard_map/ppermute | solution.py:74
  112.8 8.8 %collective-permute-start.7 = (bf16[2,1,2,104,1408]{4,3,2,1,0:T(8,128)(2,1)S(1)}, bf16[2,1,2,104,1408]{4,3,2,1,0:T(8,128)(2,1)S(1)}, u32[]{:S(2)}, u32[]{:S(2)}) collective-permute-start(bf16[2,1,2,104,1408]{4,3,2,1,0:T(8,128)(2,1)S(1)} %fusion.84), channel_id=1, source_target_pairs={{0,8},{8,0},{16,24},{24,16},{1,9},{9,1},{17,25},{25,17},{2,10},{10... | collective-permute-start | bytes 3514376 | tf_op jit(solution)/shard_map/ppermute | solution.py:74
  113.1 9.6 %collective-permute-start.9 = (bf16[2,1,2,104,1408]{4,3,2,1,0:T(8,128)(2,1)S(1)}, bf16[2,1,2,104,1408]{4,3,2,1,0:T(8,128)(2,1)S(1)}, u32[]{:S(2)}, u32[]{:S(2)}) collective-permute-start(bf16[2,1,2,104,1408]{4,3,2,1,0:T(8,128)(2,1)S(1)} %fusion.81), channel_id=1, source_target_pairs={{0,8},{8,0},{16,24},{24,16},{1,9},{9,1},{17,25},{25,17},{2,10},{10... | collective-permute-start | bytes 3514376 | tf_op jit(solution)/shard_map/ppermute | solution.py:74
  113.4 10.7 %collective-permute-start.14 = (bf16[2,1,2,104,1408]{4,3,2,1,0:T(8,128)(2,1)}, bf16[2,1,2,104,1408]{4,3,2,1,0:T(8,128)(2,1)S(1)}, u32[]{:S(2)}, u32[]{:S(2)}) collective-permute-start(bf16[2,1,2,104,1408]{4,3,2,1,0:T(8,128)(2,1)} %fusion.78), channel_id=1, source_target_pairs={{0,8},{8,0},{16,24},{24,16},{1,9},{9,1},{17,25},{25,17},{2,10},{10... | collective-permute-start | bytes 3514376 | tf_op jit(solution)/shard_map/ppermute | solution.py:74
  115.5 10.9 %collective-permute-start.16 = (bf16[2,1,2,104,1408]{4,3,2,1,0:T(8,128)(2,1)}, bf16[2,1,2,104,1408]{4,3,2,1,0:T(8,128)(2,1)S(1)}, u32[]{:S(2)}, u32[]{:S(2)}) collective-permute-start(bf16[2,1,2,104,1408]{4,3,2,1,0:T(8,128)(2,1)} %fusion.75), channel_id=1, source_target_pairs={{0,8},{8,0},{16,24},{24,16},{1,9},{9,1},{17,25},{25,17},{2,10},{10... | collective-permute-start | bytes 3514376 | tf_op jit(solution)/shard_map/ppermute | solution.py:74
  120.3 7.7 %collective-permute-start.21 = (bf16[2,1,2,104,1408]{4,3,2,1,0:T(8,128)(2,1)}, bf16[2,1,2,104,1408]{4,3,2,1,0:T(8,128)(2,1)S(1)}, u32[]{:S(2)}, u32[]{:S(2)}) collective-permute-start(bf16[2,1,2,104,1408]{4,3,2,1,0:T(8,128)(2,1)} %fusion.72), channel_id=1, source_target_pairs={{0,8},{8,0},{16,24},{24,16},{1,9},{9,1},{17,25},{25,17},{2,10},{10... | collective-permute-start | bytes 3514376 | tf_op jit(solution)/shard_map/ppermute | solution.py:74
  121.6 8.9 %collective-permute-start.23 = (bf16[2,1,2,104,1408]{4,3,2,1,0:T(8,128)(2,1)}, bf16[2,1,2,104,1408]{4,3,2,1,0:T(8,128)(2,1)S(1)}, u32[]{:S(2)}, u32[]{:S(2)}) collective-permute-start(bf16[2,1,2,104,1408]{4,3,2,1,0:T(8,128)(2,1)} %fusion.69), channel_id=1, source_target_pairs={{0,8},{8,0},{16,24},{24,16},{1,9},{9,1},{17,25},{25,17},{2,10},{10... | collective-permute-start | bytes 3514376 | tf_op jit(solution)/shard_map/ppermute | solution.py:74
  122.8 9.4 %collective-permute-start.2 = (bf16[2,1,2,104,1408]{4,3,2,1,0:T(8,128)(2,1)S(1)}, bf16[2,1,2,104,1408]{4,3,2,1,0:T(8,128)(2,1)S(1)}, u32[]{:S(2)}, u32[]{:S(2)}) collective-permute-start(bf16[2,1,2,104,1408]{4,3,2,1,0:T(8,128)(2,1)S(1)} %fusion.87), channel_id=1, source_target_pairs={{0,8},{8,0},{16,24},{24,16},{1,9},{9,1},{17,25},{25,17},{2,10},{10... | collective-permute-start | bytes 3514376 | tf_op jit(solution)/shard_map/ppermute | solution.py:74
  124.0 91.9 %collective-permute-start.1 = (bf16[1,2,104,1408]{3,2,1,0:T(8,128)(2,1)S(1)}, bf16[1,2,104,1408]{3,2,1,0:T(8,128)(2,1)S(1)}, u32[]{:S(2)}, u32[]{:S(2)}) collective-permute-start(bf16[1,2,104,1408]{3,2,1,0:T(8,128)(2,1)S(1)} %fusion.173), channel_id=1, source_target_pairs={{0,16},{8,24},{16,0},{24,8},{1,17},{9,25},{17,1},{25,9},{2,18},{10... | collective-permute-start | bytes 1757192 | tf_op jit(solution)/shard_map/ppermute | solution.py:76
  126.5 26.3 %collective-permute-start.8 = (bf16[1,2,104,1408]{3,2,1,0:T(8,128)(2,1)S(1)}, bf16[1,2,104,1408]{3,2,1,0:T(8,128)(2,1)S(1)}, u32[]{:S(2)}, u32[]{:S(2)}) collective-permute-start(bf16[1,2,104,1408]{3,2,1,0:T(8,128)(2,1)S(1)} %fusion.175), channel_id=1, source_target_pairs={{0,16},{8,24},{16,0},{24,8},{1,17},{9,25},{17,1},{25,9},{2,18},{10... | collective-permute-start | bytes 1757192 | tf_op jit(solution)/shard_map/ppermute | solution.py:76
  128.0 37.3 %collective-permute-start.10 = (bf16[1,2,104,1408]{3,2,1,0:T(8,128)(2,1)S(1)}, bf16[1,2,104,1408]{3,2,1,0:T(8,128)(2,1)S(1)}, u32[]{:S(2)}, u32[]{:S(2)}) collective-permute-start(bf16[1,2,104,1408]{3,2,1,0:T(8,128)(2,1)S(1)} %fusion.176), channel_id=1, source_target_pairs={{0,16},{8,24},{16,0},{24,8},{1,17},{9,25},{17,1},{25,9},{2,18},{10... | collective-permute-start | bytes 1757192 | tf_op jit(solution)/shard_map/ppermute | solution.py:76
  130.6 47.3 %collective-permute-start.15 = (bf16[1,2,104,1408]{3,2,1,0:T(8,128)(2,1)S(1)}, bf16[1,2,104,1408]{3,2,1,0:T(8,128)(2,1)S(1)}, u32[]{:S(2)}, u32[]{:S(2)}) collective-permute-start(bf16[1,2,104,1408]{3,2,1,0:T(8,128)(2,1)S(1)} %fusion.177), channel_id=1, source_target_pairs={{0,16},{8,24},{16,0},{24,8},{1,17},{9,25},{17,1},{25,9},{2,18},{10... | collective-permute-start | bytes 1757192 | tf_op jit(solution)/shard_map/ppermute | solution.py:76
  132.2 58.2 %collective-permute-start.17 = (bf16[1,2,104,1408]{3,2,1,0:T(8,128)(2,1)S(1)}, bf16[1,2,104,1408]{3,2,1,0:T(8,128)(2,1)S(1)}, u32[]{:S(2)}, u32[]{:S(2)}) collective-permute-start(bf16[1,2,104,1408]{3,2,1,0:T(8,128)(2,1)S(1)} %fusion.178), channel_id=1, source_target_pairs={{0,16},{8,24},{16,0},{24,8},{1,17},{9,25},{17,1},{25,9},{2,18},{10... | collective-permute-start | bytes 1757192 | tf_op jit(solution)/shard_map/ppermute | solution.py:76
  152.7 50.2 %collective-permute-start.22 = (bf16[1,2,104,1408]{3,2,1,0:T(8,128)(2,1)S(1)}, bf16[1,2,104,1408]{3,2,1,0:T(8,128)(2,1)S(1)}, u32[]{:S(2)}, u32[]{:S(2)}) collective-permute-start(bf16[1,2,104,1408]{3,2,1,0:T(8,128)(2,1)S(1)} %fusion.179), channel_id=1, source_target_pairs={{0,16},{8,24},{16,0},{24,8},{1,17},{9,25},{17,1},{25,9},{2,18},{10... | collective-permute-start | bytes 1757192 | tf_op jit(solution)/shard_map/ppermute | solution.py:76
  165.3 50.2 %collective-permute-start.24 = (bf16[1,2,104,1408]{3,2,1,0:T(8,128)(2,1)S(1)}, bf16[1,2,104,1408]{3,2,1,0:T(8,128)(2,1)S(1)}, u32[]{:S(2)}, u32[]{:S(2)}) collective-permute-start(bf16[1,2,104,1408]{3,2,1,0:T(8,128)(2,1)S(1)} %fusion.180), channel_id=1, source_target_pairs={{0,16},{8,24},{16,0},{24,8},{1,17},{9,25},{17,1},{25,9},{2,18},{10... | collective-permute-start | bytes 1757192 | tf_op jit(solution)/shard_map/ppermute | solution.py:76
  177.8 50.2 %collective-permute-start.3 = (bf16[1,2,104,1408]{3,2,1,0:T(8,128)(2,1)S(1)}, bf16[1,2,104,1408]{3,2,1,0:T(8,128)(2,1)S(1)}, u32[]{:S(2)}, u32[]{:S(2)}) collective-permute-start(bf16[1,2,104,1408]{3,2,1,0:T(8,128)(2,1)S(1)} %fusion.174), channel_id=1, source_target_pairs={{0,16},{8,24},{16,0},{24,8},{1,17},{9,25},{17,1},{25,9},{2,18},{10... | collective-permute-start | bytes 1757192 | tf_op jit(solution)/shard_map/ppermute | solution.py:76
  190.4 87.3 %collective-permute-start.12 = (bf16[1,2,104,1408]{3,2,1,0:T(8,128)(2,1)S(1)}, bf16[1,2,104,1408]{3,2,1,0:T(8,128)(2,1)S(1)}, u32[]{:S(2)}, u32[]{:S(2)}) collective-permute-start(bf16[1,2,104,1408]{3,2,1,0:T(8,128)(2,1)S(1)} %fusion.164), channel_id=1, source_target_pairs={{0,8},{8,0},{16,24},{24,16},{1,9},{9,1},{17,25},{25,17},{2,10},{10... | collective-permute-start | bytes 1757192 | tf_op jit(solution)/shard_map/ppermute | solution.py:82
  190.4 88.1 %slice-start.6 = ((s8[11534336]{0:T(1024)(128)(4,1)}), s8[4194304]{0:T(1024)(128)(4,1)S(1)}, s32[]{:S(2)}) async-start(s8[11534336]{0:T(1024)(128)(4,1)} %bitcast.496), calls=%async_computation.11 | async-start | bytes 8388608
  190.8 87.7 %slice-start.7 = ((s8[11534336]{0:T(1024)(128)(4,1)}), s8[4194304]{0:T(1024)(128)(4,1)S(1)}, s32[]{:S(2)}) async-start(s8[11534336]{0:T(1024)(128)(4,1)} %bitcast.496), calls=%async_computation.12 | async-start | bytes 8388608
  202.9 37.7 %collective-permute-start.11 = (bf16[1,2,104,1408]{3,2,1,0:T(8,128)(2,1)S(1)}, bf16[1,2,104,1408]{3,2,1,0:T(8,128)(2,1)S(1)}, u32[]{:S(2)}, u32[]{:S(2)}) collective-permute-start(bf16[1,2,104,1408]{3,2,1,0:T(8,128)(2,1)S(1)} %fusion.164), channel_id=1, source_target_pairs={{0,16},{8,24},{16,0},{24,8},{1,17},{9,25},{17,1},{25,9},{2,18},{10... | collective-permute-start | bytes 1757192 | tf_op jit(solution)/shard_map/ppermute | solution.py:80
  215.5 64.5 %collective-permute-start.19 = (bf16[1,2,104,1408]{3,2,1,0:T(8,128)(2,1)S(1)}, bf16[1,2,104,1408]{3,2,1,0:T(8,128)(2,1)S(1)}, u32[]{:S(2)}, u32[]{:S(2)}) collective-permute-start(bf16[1,2,104,1408]{3,2,1,0:T(8,128)(2,1)S(1)} %fusion.160), channel_id=1, source_target_pairs={{0,8},{8,0},{16,24},{24,16},{1,9},{9,1},{17,25},{25,17},{2,10},{10... | collective-permute-start | bytes 1757192 | tf_op jit(solution)/shard_map/ppermute | solution.py:82
  215.9 37.2 %collective-permute-start.18 = (bf16[1,2,104,1408]{3,2,1,0:T(8,128)(2,1)S(1)}, bf16[1,2,104,1408]{3,2,1,0:T(8,128)(2,1)S(1)}, u32[]{:S(2)}, u32[]{:S(2)}) collective-permute-start(bf16[1,2,104,1408]{3,2,1,0:T(8,128)(2,1)S(1)} %fusion.160), channel_id=1, source_target_pairs={{0,16},{8,24},{16,0},{24,8},{1,17},{9,25},{17,1},{25,9},{2,18},{10... | collective-permute-start | bytes 1757192 | tf_op jit(solution)/shard_map/ppermute | solution.py:80
  228.1 37.7 %collective-permute-start.25 = (bf16[1,2,104,1408]{3,2,1,0:T(8,128)(2,1)S(1)}, bf16[1,2,104,1408]{3,2,1,0:T(8,128)(2,1)S(1)}, u32[]{:S(2)}, u32[]{:S(2)}) collective-permute-start(bf16[1,2,104,1408]{3,2,1,0:T(8,128)(2,1)S(1)} %fusion.156), channel_id=1, source_target_pairs={{0,16},{8,24},{16,0},{24,8},{1,17},{9,25},{17,1},{25,9},{2,18},{10... | collective-permute-start | bytes 1757192 | tf_op jit(solution)/shard_map/ppermute | solution.py:80
  240.6 36.9 %collective-permute-start.4 = (bf16[1,2,104,1408]{3,2,1,0:T(8,128)(2,1)S(1)}, bf16[1,2,104,1408]{3,2,1,0:T(8,128)(2,1)S(1)}, u32[]{:S(2)}, u32[]{:S(2)}) collective-permute-start(bf16[1,2,104,1408]{3,2,1,0:T(8,128)(2,1)S(1)} %fusion.168), channel_id=1, source_target_pairs={{0,16},{8,24},{16,0},{24,8},{1,17},{9,25},{17,1},{25,9},{2,18},{10... | collective-permute-start | bytes 1757192 | tf_op jit(solution)/shard_map/ppermute | solution.py:80
  253.2 25.1 %collective-permute-start.13 = (bf16[1,2,104,1408]{3,2,1,0:T(8,128)(2,1)S(1)}, bf16[1,2,104,1408]{3,2,1,0:T(8,128)(2,1)S(1)}, u32[]{:S(2)}, u32[]{:S(2)}) collective-permute-start(bf16[1,2,104,1408]{3,2,1,0:T(8,128)(2,1)S(1)} %collective-permute-done.11), channel_id=1, source_target_pairs={{0,8},{8,0},{16,24},{24,16},{1,9},{9,1},{17,25},{25,17},{2,10},{10... | collective-permute-start | bytes 1757192 | tf_op jit(solution)/shard_map/ppermute | solution.py:82
  265.7 16.5 %collective-permute-start.26 = (bf16[1,2,104,1408]{3,2,1,0:T(8,128)(2,1)S(1)}, bf16[1,2,104,1408]{3,2,1,0:T(8,128)(2,1)S(1)}, u32[]{:S(2)}, u32[]{:S(2)}) collective-permute-start(bf16[1,2,104,1408]{3,2,1,0:T(8,128)(2,1)S(1)} %fusion.156), channel_id=1, source_target_pairs={{0,8},{8,0},{16,24},{24,16},{1,9},{9,1},{17,25},{25,17},{2,10},{10... | collective-permute-start | bytes 1757192 | tf_op jit(solution)/shard_map/ppermute | solution.py:82
  277.6 6.5 %collective-permute-start.5 = (bf16[1,2,104,1408]{3,2,1,0:T(8,128)(2,1)S(1)}, bf16[1,2,104,1408]{3,2,1,0:T(8,128)(2,1)S(1)}, u32[]{:S(2)}, u32[]{:S(2)}) collective-permute-start(bf16[1,2,104,1408]{3,2,1,0:T(8,128)(2,1)S(1)} %fusion.168), channel_id=1, source_target_pairs={{0,8},{8,0},{16,24},{24,16},{1,9},{9,1},{17,25},{25,17},{2,10},{10... | collective-permute-start | bytes 1757192 | tf_op jit(solution)/shard_map/ppermute | solution.py:82
  277.7 2.9 collective-permute-start.20
  278.3 3.9 collective-permute-start.27
  280.0 4.0 collective-permute-start.6
  (10 other events, 98.5 us)
Sparse Core Ops, SparseCore 0:
  21.3 74.9 all-gather.3
  302.2 86.3 reduce-scatter.1
